TPU v7x, 512 devices: a whole 4x4x16 slice. The times are simulated.
512 devices in a mesh: feat: 8 (over x, core), vert: 64 (over y, z).
Axes of the slice: x: 4, y: 4, z: 16, core: 2. Of those that a mesh axis runs over, the one named last changes fastest.
Arguments:
- features: bfloat16 [512, 131072], P('feat', 'vert'), may hold values from -6 to 6
- tiles: bfloat16 [64, 56, 128, 128], P('vert'), may hold values from -0.375 to 0.375
- tile_rows: int32 [64, 56], P('vert'), may hold values from 0 to 15, as said below
- tile_cols: int32 [64, 56], P('vert'), may hold values from 0 to 1023, as said below
- tile_counts: int32 [64], P('vert'), may hold values from 1 to 56, as said below
- weight: bfloat16 [512, 512], replicated, may hold values from -0.25 to 0.25
- output_gradient: bfloat16 [512, 131072], P(None, ('vert', 'feat')), may hold values from -6 to 6
Outputs:
- activation: bfloat16 [512, 131072], P(None, ('vert', 'feat'))
- weight_gradient: float32 [512, 512], replicated
- feature_grad: bfloat16 [512, 131072], P('feat', 'vert')
Inputs may be any that keep to these rules, and one draw needn't show every extreme that they name: `tile_rows`: slots at or beyond a block's count are unused; their tiles and indices are arbitrary. The block of a column tile, tile_cols // 16, equals the slot's own block or differs from it in exactly one of the lowest 4 bits. `tile_counts`: some block uses all 56 slots.
All inputs are finite; a program needn't handle non-finite values.
Results may differ from a plain program's by a relative error of at most 0.02.
Values may be sent and summed in bfloat16 or wider, within the bound.
A program may use at most 64 MiB of HBM per device.

v0:
```python
import jax
import jax.numpy as jnp
from jax import lax
from jax.sharding import PartitionSpec as P

LEVELS = 4


def partner(shard, axis, stride):
    return lax.ppermute(shard, axis, [(i, i ^ 1 << stride) for i in range(lax.axis_size(axis))])


def fetch_partners(features):
    fetched = []
    for bit in range(LEVELS):
        fetched.append(partner(features, "vert", bit))
    return fetched


def send_partials(remote_terms):
    received = []
    for bit in range(LEVELS):
        outgoing = remote_terms[:, bit].astype(jnp.bfloat16)
        received.append(partner(outgoing, "vert", bit).astype(jnp.float32))
    return received


def tile_products(stacked, level, local, rows, block_tiles, weights, row_tiles):
    picked = stacked[level, :, local]
    share_value = jnp.einsum(
        "cfk,crk->cfr", picked, block_tiles, preferred_element_type=jnp.float32
    )
    indicator_matrix = (rows[None, :] == jnp.arange(row_tiles, dtype=jnp.int32)[:, None]).astype(
        jnp.float32
    ) * weights[None, :]
    reduced_total = jnp.einsum("zy,yqw->qzw", indicator_matrix, share_value)
    return reduced_total.reshape(stacked.shape[1], row_tiles * stacked.shape[3])


def position_summands(share_value, slot_index, groups, feat_local, vdev):
    targets = jnp.arange(groups * (vdev // share_value.shape[2]), dtype=jnp.int32)
    placing = (slot_index[None, :] == targets[:, None]).astype(jnp.float32)
    return jnp.einsum("sc,cfk->fsk", placing, share_value).reshape(feat_local, groups, vdev)


def body(features, tiles, tile_rows, tile_cols, tile_counts, weight, output_gradient):
    feat_local, vdev = features.shape
    tile_side = tiles.shape[2]
    slot_count = tiles.shape[1]
    row_tiles = vdev // tile_side
    my_block = lax.axis_index("vert")
    block_tiles = tiles[0]
    rows = tile_rows[0]
    cols = tile_cols[0]
    differ = jnp.bitwise_xor(cols // row_tiles, my_block)
    level = jnp.zeros(cols.shape, jnp.int32)
    for bit in range(LEVELS):
        level = level + jnp.where(differ == 1 << bit, bit + 1, 0).astype(jnp.int32)
    local = cols % row_tiles
    valid = (jnp.arange(slot_count, dtype=jnp.int32) < tile_counts[0]).astype(jnp.float32)
    stacked = jnp.stack([features] + fetch_partners(features)).reshape(
        LEVELS + 1, feat_local, row_tiles, tile_side
    )
    aggregated = tile_products(stacked, level, local, rows, block_tiles, valid, row_tiles).astype(
        jnp.bfloat16
    )
    full_rows = lax.all_to_all(aggregated, "feat", split_axis=1, concat_axis=0, tiled=True)
    pre = jnp.einsum("io,iv->ov", weight, full_rows, preferred_element_type=jnp.float32)
    sigma = jax.nn.sigmoid(pre)
    activation = (pre * sigma).astype(jnp.bfloat16)
    pre_grad = (output_gradient.astype(jnp.float32) * sigma * (1.0 + pre * (1.0 - sigma))).astype(
        jnp.bfloat16
    )
    weight_term = jnp.einsum("iv,ov->io", full_rows, pre_grad, preferred_element_type=jnp.float32)
    weight_gradient = lax.psum(weight_term, ("feat", "vert"))
    agg_grad = jnp.einsum("io,ov->iv", weight, pre_grad, preferred_element_type=jnp.float32).astype(
        jnp.bfloat16
    )
    grad_cols = lax.all_to_all(agg_grad, "feat", split_axis=0, concat_axis=1, tiled=True)
    picked = grad_cols.reshape(feat_local, row_tiles, tile_side)[:, rows, :]
    share_value = (
        jnp.einsum("fcr,crk->cfk", picked, block_tiles, preferred_element_type=jnp.float32)
        * valid[:, None, None]
    )
    spread = position_summands(share_value, level * row_tiles + local, LEVELS + 1, feat_local, vdev)
    received = send_partials(spread[:, 1:])
    feature_grad = spread[:, 0]
    for term in received:
        feature_grad = feature_grad + term
    return (activation, weight_gradient, feature_grad.astype(jnp.bfloat16))


def solution(mesh):
    in_specs = (
        P("feat", "vert"),
        P("vert", None, None, None),
        P("vert", None),
        P("vert", None),
        P("vert"),
        P(),
        P(None, ("vert", "feat")),
    )
    out_specs = (P(None, ("vert", "feat")), P(), P("feat", "vert"))
    return jax.shard_map(body, mesh=mesh, in_specs=in_specs, out_specs=out_specs, check_vma=False)
```

profile of v0, /device:TPU:1, one launch (start us, length us, event | category | flops | bytes accessed | tf_op | source)
XLA Modules:
  0.0 628.8 jit_solution(14471863540489969215)
XLA Ops:
  7.2 5.9 collective-permute-start.1
  13.1 3.5 collective-permute-start
  16.6 12.7 %collective-permute-start.3 = (bf16[64,2048]{1,0:T(8,128)(2,1)}, bf16[64,2048]{1,0:T(8,128)(2,1)S(1)}, u32[]{:S(2)}, u32[]{:S(2)}) collective-permute-start(bf16[64,2048]{1,0:T(8,128)(2,1)} %param.7), channel_id=1, source_target_pairs={{0,8},{1,9},{2,10},{3,11},{4,12},{5,13},{6,14},{7,15},{8,0},{9,1},... | collective-permute-start | bytes 786440 | tf_op jit(solution)/shard_map/ppermute | solution.py:10
  29.4 4.0 collective-permute-start.2
  36.6 10.2 %collective-permute-done.3 = bf16[64,2048]{1,0:T(8,128)(2,1)S(1)} collective-permute-done((bf16[64,2048]{1,0:T(8,128)(2,1)}, bf16[64,2048]{1,0:T(8,128)(2,1)S(1)}, u32[]{:S(2)}, u32[]{:S(2)}) %collective-permute-start.3) | collective-permute-done | bytes 262176 | tf_op jit(solution)/shard_map/ppermute | solution.py:10
  46.9 31.9 %collective-permute-done.2 = bf16[64,2048]{1,0:T(8,128)(2,1)S(1)} collective-permute-done((bf16[64,2048]{1,0:T(8,128)(2,1)}, bf16[64,2048]{1,0:T(8,128)(2,1)S(1)}, u32[]{:S(2)}, u32[]{:S(2)}) %collective-permute-start.2) | collective-permute-done | bytes 262176 | tf_op jit(solution)/shard_map/ppermute | solution.py:10
  81.8 2.2 gather_fusion
  86.9 4.8 all-to-all-start
  91.8 6.3 %all-to-all-done = bf16[64,8,256]{2,0,1:T(8,128)(2,1)S(1)} async-done(((bf16[64,8,256]{2,0,1:T(8,128)(2,1)}), bf16[64,8,256]{2,0,1:T(8,128)(2,1)S(1)}, u32[]{:S(2)}, u32[]{:S(2)}) %all-to-all-start) | async-done | bytes 262176 | tf_op jit(solution)/shard_map/all_to_all | solution.py:67
  100.6 4.4 all-to-all-start.1
  105.0 6.5 %all-to-all-done.1 = bf16[8,64,256]{2,1,0:T(8,128)(2,1)S(1)} async-done(((bf16[8,64,256]{2,1,0:T(8,128)(2,1)}), bf16[8,64,256]{2,1,0:T(8,128)(2,1)S(1)}, u32[]{:S(2)}, u32[]{:S(2)}) %all-to-all-start.1) | async-done | bytes 262176 | tf_op jit(solution)/shard_map/all_to_all | solution.py:79
  113.1 2.4 fusion.8
  115.5 4.4 reshape.232
  119.9 2.5 convert.6
  122.4 1.9 fusion.51
  126.3 1.9 collective-permute-start.5
  128.3 1.9 collective-permute-start.6
  130.2 8.5 %collective-permute-start.7 = (bf16[64,2048]{1,0:T(8,128)(2,1)S(1)}, bf16[64,2048]{1,0:T(8,128)(2,1)}, u32[]{:S(2)}, u32[]{:S(2)}) collective-permute-start(bf16[64,2048]{1,0:T(8,128)(2,1)S(1)} %bitcast.108), channel_id=1, source_target_pairs={{0,8},{1,9},{2,10},{3,11},{4,12},{5,13},{6,14},{7,15},{8,0},{9,1},... | collective-permute-start | bytes 786440 | tf_op jit(solution)/shard_map/ppermute | solution.py:10
  138.7 5.8 collective-permute-start.4
  145.8 1.8 copy.81
  147.7 33.5 %collective-permute-done.6 = bf16[64,2048]{1,0:T(8,128)(2,1)} collective-permute-done((bf16[64,2048]{1,0:T(8,128)(2,1)}, bf16[64,2048]{1,0:T(8,128)(2,1)}, u32[]{:S(2)}, u32[]{:S(2)}) %collective-permute-start.6) | collective-permute-done | bytes 262176 | tf_op jit(solution)/shard_map/ppermute | solution.py:10
  181.2 2.2 fusion.25
  183.3 436.4 %all-reduce.2.cloned.1.call-done = f32[512,512]{1,0:T(8,128)} async-done(((f32[512,512]{1,0:T(8,128)}), f32[512,512]{1,0:T(8,128)}) %all-reduce.2.cloned.1.call-update) | async-done | bytes 1048592 | tf_op jit(solution)/shard_map/psum | solution.py:75
  619.7 2.3 copy.122
  (52 shorter events, 16.0 us)
Async XLA Ops:
  7.2 76.9 %copy-start = (bf16[1,56,128,128]{3,2,1,0:T(8,128)(2,1)S(1)}, bf16[1,56,128,128]{3,2,1,0:T(8,128)(2,1)}, u32[]{:S(2)}) copy-start(bf16[1,56,128,128]{3,2,1,0:T(8,128)(2,1)} %param.8) | copy-start | bytes 5505028
  7.2 29.3 %collective-permute-start.1 = (bf16[64,2048]{1,0:T(8,128)(2,1)}, bf16[64,2048]{1,0:T(8,128)(2,1)S(1)}, u32[]{:S(2)}, u32[]{:S(2)}) collective-permute-start(bf16[64,2048]{1,0:T(8,128)(2,1)} %param.7), channel_id=1, source_target_pairs={{0,2},{1,3},{2,0},{3,1},{4,6},{5,7},{6,4},{7,5},{8,10},{9,11},{10,... | collective-permute-start | bytes 786440 | tf_op jit(solution)/shard_map/ppermute | solution.py:10
  13.1 23.5 %collective-permute-start = (bf16[64,2048]{1,0:T(8,128)(2,1)}, bf16[64,2048]{1,0:T(8,128)(2,1)S(1)}, u32[]{:S(2)}, u32[]{:S(2)}) collective-permute-start(bf16[64,2048]{1,0:T(8,128)(2,1)} %param.7), channel_id=1, source_target_pairs={{0,1},{1,0},{2,3},{3,2},{4,5},{5,4},{6,7},{7,6},{8,9},{9,8},{10,11... | collective-permute-start | bytes 786440 | tf_op jit(solution)/shard_map/ppermute | solution.py:10
  16.6 30.2 %collective-permute-start.3 = (bf16[64,2048]{1,0:T(8,128)(2,1)}, bf16[64,2048]{1,0:T(8,128)(2,1)S(1)}, u32[]{:S(2)}, u32[]{:S(2)}) collective-permute-start(bf16[64,2048]{1,0:T(8,128)(2,1)} %param.7), channel_id=1, source_target_pairs={{0,8},{1,9},{2,10},{3,11},{4,12},{5,13},{6,14},{7,15},{8,0},{9,1},... | collective-permute-start | bytes 786440 | tf_op jit(solution)/shard_map/ppermute | solution.py:10
  29.4 49.4 %collective-permute-start.2 = (bf16[64,2048]{1,0:T(8,128)(2,1)}, bf16[64,2048]{1,0:T(8,128)(2,1)S(1)}, u32[]{:S(2)}, u32[]{:S(2)}) collective-permute-start(bf16[64,2048]{1,0:T(8,128)(2,1)} %param.7), channel_id=1, source_target_pairs={{0,4},{1,5},{2,6},{3,7},{4,0},{5,1},{6,2},{7,3},{8,12},{9,13},{10,... | collective-permute-start | bytes 786440 | tf_op jit(solution)/shard_map/ppermute | solution.py:10
  84.0 1.4 copy-start.3
  85.4 6.2 copy-start.2
  86.0 12.1 %copy-start.1 = (bf16[512,512]{1,0:T(8,128)(2,1)S(1)}, bf16[512,512]{1,0:T(8,128)(2,1)}, u32[]{:S(2)}) copy-start(bf16[512,512]{1,0:T(8,128)(2,1)} %param.12) | copy-start | bytes 1572868
  86.9 11.3 %all-to-all-start = ((bf16[64,8,256]{2,0,1:T(8,128)(2,1)}), bf16[64,8,256]{2,0,1:T(8,128)(2,1)S(1)}, u32[]{:S(2)}, u32[]{:S(2)}) async-start(bf16[64,8,256]{2,0,1:T(8,128)(2,1)} %copy.75), calls=%async_computation | async-start | bytes 524288 | tf_op jit(solution)/shard_map/all_to_all | solution.py:67
  99.4 5.6 copy-start.4
  100.6 10.9 %all-to-all-start.1 = ((bf16[8,64,256]{2,1,0:T(8,128)(2,1)}), bf16[8,64,256]{2,1,0:T(8,128)(2,1)S(1)}, u32[]{:S(2)}, u32[]{:S(2)}) async-start(bf16[8,64,256]{2,1,0:T(8,128)(2,1)} %bitcast.12), calls=%async_computation.1 | async-start | bytes 524288 | tf_op jit(solution)/shard_map/all_to_all | solution.py:79
  104.9 514.8 %all-reduce.2.cloned.1.call-start = ((), (), s32[]{:S(2)}) async-start(), calls=%async_computation.2 | async-start | bytes 2097152 | tf_op jit(solution)/shard_map/psum | solution.py:75
  126.3 21.3 %collective-permute-start.5 = (bf16[64,2048]{1,0:T(8,128)(2,1)}, bf16[64,2048]{1,0:T(8,128)(2,1)}, u32[]{:S(2)}, u32[]{:S(2)}) collective-permute-start(bf16[64,2048]{1,0:T(8,128)(2,1)} %bitcast.96), channel_id=1, source_target_pairs={{0,2},{1,3},{2,0},{3,1},{4,6},{5,7},{6,4},{7,5},{8,10},{9,11},{10,... | collective-permute-start | bytes 786440 | tf_op jit(solution)/shard_map/ppermute | solution.py:10
  128.3 52.9 %collective-permute-start.6 = (bf16[64,2048]{1,0:T(8,128)(2,1)}, bf16[64,2048]{1,0:T(8,128)(2,1)}, u32[]{:S(2)}, u32[]{:S(2)}) collective-permute-start(bf16[64,2048]{1,0:T(8,128)(2,1)} %bitcast.95), channel_id=1, source_target_pairs={{0,4},{1,5},{2,6},{3,7},{4,0},{5,1},{6,2},{7,3},{8,12},{9,13},{10,... | collective-permute-start | bytes 786440 | tf_op jit(solution)/shard_map/ppermute | solution.py:10
  130.2 50.9 %collective-permute-start.7 = (bf16[64,2048]{1,0:T(8,128)(2,1)S(1)}, bf16[64,2048]{1,0:T(8,128)(2,1)}, u32[]{:S(2)}, u32[]{:S(2)}) collective-permute-start(bf16[64,2048]{1,0:T(8,128)(2,1)S(1)} %bitcast.108), channel_id=1, source_target_pairs={{0,8},{1,9},{2,10},{3,11},{4,12},{5,13},{6,14},{7,15},{8,0},{9,1},... | collective-permute-start | bytes 786440 | tf_op jit(solution)/shard_map/ppermute | solution.py:10
  138.7 42.4 %collective-permute-start.4 = (bf16[64,2048]{1,0:T(8,128)(2,1)S(1)}, bf16[64,2048]{1,0:T(8,128)(2,1)}, u32[]{:S(2)}, u32[]{:S(2)}) collective-permute-start(bf16[64,2048]{1,0:T(8,128)(2,1)S(1)} %bitcast.107), channel_id=1, source_target_pairs={{0,1},{1,0},{2,3},{3,2},{4,5},{5,4},{6,7},{7,6},{8,9},{9,8},{10,11... | collective-permute-start | bytes 786440 | tf_op jit(solution)/shard_map/ppermute | solution.py:10
  145.8 35.3 %slice-start = ((f32[64,5,2048]{2,1,0:T(8,128)}), f32[64,1,2048]{2,1,0:T(1,128)S(1)}, s32[]{:S(2)}) async-start(f32[64,5,2048]{2,1,0:T(8,128)} %reshape.232), calls=%async_computation.3 | async-start | bytes 1048576 | tf_op jit(solution)/shard_map/slice | solution.py:87
Sparse Core Ops, SparseCore 0:
  146.0 473.7 all-reduce.1
where the time goes:
time: 630 us; the launch traced here: 629 us
  waiting for transfers between devices  525 us (83%)
  starting transfers between devices  53.5 us (8%)
  local copies, waits for them, and re-layouts  22.5 us (4%)
  between operations  14.9 us (2%)
  matrix products  7.74 us (1%)
    psum x1, waiting for transfers between devices, body(): weight_gradient = lax.psum(weight_term, ('feat', 'vert'))  436 us
    ppermute x8, waiting for transfers between devices, partner(): lax.ppermute(shard, axis, [(i, i ^ 1 << stride) for i in range(lax.axis_s...  75.5 us
    ppermute x8, starting transfers between devices, partner(): lax.ppermute(shard, axis, [(i, i ^ 1 << stride) for i in range(lax.axis_s...  44.3 us
  transfers between devices with their start and end apart: 11, of which 6 were waited for; matrix products, arithmetic and copies ran while one was open for 1% of the time, Pallas kernels for 0%

commit v1 on v0

--- a/solution.py
+++ b/solution.py
@@ -72,7 +72,7 @@
         jnp.bfloat16
     )
     weight_term = jnp.einsum("iv,ov->io", full_rows, pre_grad, preferred_element_type=jnp.float32)
-    weight_gradient = lax.psum(weight_term, ("feat", "vert"))
+    weight_gradient = lax.psum(lax.psum(weight_term, "feat"), "vert")
     agg_grad = jnp.einsum("io,ov->iv", weight, pre_grad, preferred_element_type=jnp.float32).astype(
         jnp.bfloat16
     )

time: 630 us -> 504 us (0.80); the launches traced: 629 us -> 494 us
  waiting for transfers between devices: 525 us -> 383 us
    psum x1 -> x2, waiting for transfers between devices: 436 us -> 301 us  [body(): weight_gradient = lax.psum(lax.psum(weight_term, 'feat'), 'vert')]
  transfers between devices with their start and end apart: 11 -> 12, of which waited for: 6 -> 9; matrix products, arithmetic and copies ran while one was open for 1% -> 6% of each run, Pallas kernels for 0% -> 0%
where the time goes in v1:
time: 504 us; the launch traced here: 494 us
  waiting for transfers between devices  383 us (76%)
  starting transfers between devices  54.6 us (11%)
  local copies, waits for them, and re-layouts  26.7 us (5%)
  between operations  15 us (3%)
  matrix products  7.74 us (2%)
  other arithmetic  7.34 us (1%)
    psum x2, waiting for transfers between devices, body(): weight_gradient = lax.psum(lax.psum(weight_term, 'feat'), 'vert')  301 us
    ppermute x8, waiting for transfers between devices, partner(): lax.ppermute(shard, axis, [(i, i ^ 1 << stride) for i in range(lax.axis_s...  70 us
    ppermute x8, starting transfers between devices, partner(): lax.ppermute(shard, axis, [(i, i ^ 1 << stride) for i in range(lax.axis_s...  45.5 us
    unnamed x26, local copies, waits for them, and re-layouts  10.5 us
  transfers between devices with their start and end apart: 12, of which 9 were waited for; matrix products, arithmetic and copies ran while one was open for 6% of the time, Pallas kernels for 0%

profile of v1, /device:TPU:1, one launch (start us, length us, event | category | flops | bytes accessed | tf_op | source)
XLA Modules:
  0.0 493.9 jit_solution(3093545909105069278)
XLA Ops:
  7.2 5.9 %collective-permute-start.1 = (bf16[64,2048]{1,0:T(8,128)(2,1)}, bf16[64,2048]{1,0:T(8,128)(2,1)S(1)}, u32[]{:S(2)}, u32[]{:S(2)}) collective-permute-start(bf16[64,2048]{1,0:T(8,128)(2,1)} %param.7), channel_id=1, source_target_pairs={{0,2},{1,3},{2,0},{3,1},{4,6},{5,7},{6,4},{7,5},{8,10},{9,11},{10,... | collective-permute-start | bytes 786440 | tf_op jit(solution)/shard_map/ppermute | solution.py:10
  13.1 3.5 collective-permute-start
  16.6 12.7 %collective-permute-start.3 = (bf16[64,2048]{1,0:T(8,128)(2,1)}, bf16[64,2048]{1,0:T(8,128)(2,1)S(1)}, u32[]{:S(2)}, u32[]{:S(2)}) collective-permute-start(bf16[64,2048]{1,0:T(8,128)(2,1)} %param.7), channel_id=1, source_target_pairs={{0,8},{1,9},{2,10},{3,11},{4,12},{5,13},{6,14},{7,15},{8,0},{9,1},... | collective-permute-start | bytes 786440 | tf_op jit(solution)/shard_map/ppermute | solution.py:10
  29.4 4.0 collective-permute-start.2
  37.2 9.6 %collective-permute-done.3 = bf16[64,2048]{1,0:T(8,128)(2,1)S(1)} collective-permute-done((bf16[64,2048]{1,0:T(8,128)(2,1)}, bf16[64,2048]{1,0:T(8,128)(2,1)S(1)}, u32[]{:S(2)}, u32[]{:S(2)}) %collective-permute-start.3) | collective-permute-done | bytes 262176 | tf_op jit(solution)/shard_map/ppermute | solution.py:10
  46.9 31.9 %collective-permute-done.2 = bf16[64,2048]{1,0:T(8,128)(2,1)S(1)} collective-permute-done((bf16[64,2048]{1,0:T(8,128)(2,1)}, bf16[64,2048]{1,0:T(8,128)(2,1)S(1)}, u32[]{:S(2)}, u32[]{:S(2)}) %collective-permute-start.2) | collective-permute-done | bytes 262176 | tf_op jit(solution)/shard_map/ppermute | solution.py:10
  86.9 4.8 all-to-all-start
  91.9 6.3 %all-to-all-done = bf16[64,8,256]{2,0,1:T(8,128)(2,1)S(1)} async-done(((bf16[64,8,256]{2,0,1:T(8,128)(2,1)}), bf16[64,8,256]{2,0,1:T(8,128)(2,1)S(1)}, u32[]{:S(2)}, u32[]{:S(2)}) %all-to-all-start) | async-done | bytes 262176 | tf_op jit(solution)/shard_map/all_to_all | solution.py:67
  100.6 4.4 all-to-all-start.1
  106.3 5.2 %all-to-all-done.1 = bf16[8,64,256]{2,1,0:T(8,128)(2,1)S(1)} async-done(((bf16[8,64,256]{2,1,0:T(8,128)(2,1)}), bf16[8,64,256]{2,1,0:T(8,128)(2,1)S(1)}, u32[]{:S(2)}, u32[]{:S(2)}) %all-to-all-start.1) | async-done | bytes 262176 | tf_op jit(solution)/shard_map/all_to_all | solution.py:79
  113.1 2.4 fusion.8
  115.5 4.4 reshape.232
  119.9 4.0 convert.6
  123.8 57.1 %all-reduce.3.cloned.1.call-done = f32[512,512]{1,0:T(8,128)} async-done(((f32[512,512]{1,0:T(8,128)}), f32[512,512]{1,0:T(8,128)}) %all-reduce.3.cloned.1.call-update) | async-done | bytes 1048592 | tf_op jit(solution)/shard_map/psum | solution.py:75
  180.9 6.2 %fusion.51 = (bf16[64,1,2048]{2,1,0:T(2,128)(2,1)S(1)}, bf16[64,1,2048]{2,1,0:T(2,128)(2,1)S(1)}, bf16[64,1,2048]{2,1,0:T(2,128)(2,1)S(1)}, bf16[64,1,2048]{2,1,0:T(2,128)(2,1)S(1)}) fusion(bf16[64,5,2048]{2,1,0:T(8,128)(2,1)} %convert.6), kind=kLoop, calls=%fused_computation.85 | loop fusion | bytes 2097152 | tf_op jit(solution)/shard_map/slice | solution.py:23
  189.2 3.7 collective-permute-start.5
  192.9 7.4 %collective-permute-start.6 = (bf16[64,2048]{1,0:T(8,128)(2,1)}, bf16[64,2048]{1,0:T(8,128)(2,1)S(1)}, u32[]{:S(2)}, u32[]{:S(2)}) collective-permute-start(bf16[64,2048]{1,0:T(8,128)(2,1)} %bitcast.95), channel_id=1, source_target_pairs={{0,4},{1,5},{2,6},{3,7},{4,0},{5,1},{6,2},{7,3},{8,12},{9,13},{10,... | collective-permute-start | bytes 786440 | tf_op jit(solution)/shard_map/ppermute | solution.py:10
  200.3 5.9 %collective-permute-start.7 = (bf16[64,2048]{1,0:T(8,128)(2,1)S(1)}, bf16[64,2048]{1,0:T(8,128)(2,1)}, u32[]{:S(2)}, u32[]{:S(2)}) collective-permute-start(bf16[64,2048]{1,0:T(8,128)(2,1)S(1)} %bitcast.108), channel_id=1, source_target_pairs={{0,8},{1,9},{2,10},{3,11},{4,12},{5,13},{6,14},{7,15},{8,0},{9,1},... | collective-permute-start | bytes 786440 | tf_op jit(solution)/shard_map/ppermute | solution.py:10
  206.2 2.3 collective-permute-start.4
  210.3 9.1 %collective-permute-done.5 = bf16[64,2048]{1,0:T(8,128)(2,1)S(1)} collective-permute-done((bf16[64,2048]{1,0:T(8,128)(2,1)}, bf16[64,2048]{1,0:T(8,128)(2,1)S(1)}, u32[]{:S(2)}, u32[]{:S(2)}) %collective-permute-start.5) | collective-permute-done | bytes 262176 | tf_op jit(solution)/shard_map/ppermute | solution.py:10
  219.4 10.8 %collective-permute-done.6 = bf16[64,2048]{1,0:T(8,128)(2,1)S(1)} collective-permute-done((bf16[64,2048]{1,0:T(8,128)(2,1)}, bf16[64,2048]{1,0:T(8,128)(2,1)S(1)}, u32[]{:S(2)}, u32[]{:S(2)}) %collective-permute-start.6) | collective-permute-done | bytes 262176 | tf_op jit(solution)/shard_map/ppermute | solution.py:10
  230.2 8.6 %collective-permute-done.4 = bf16[64,2048]{1,0:T(8,128)(2,1)} collective-permute-done((bf16[64,2048]{1,0:T(8,128)(2,1)S(1)}, bf16[64,2048]{1,0:T(8,128)(2,1)}, u32[]{:S(2)}, u32[]{:S(2)}) %collective-permute-start.4) | collective-permute-done | bytes 262176 | tf_op jit(solution)/shard_map/ppermute | solution.py:10
  240.9 243.9 %all-reduce.5.cloned.1.call-done = f32[512,512]{1,0:T(8,128)} async-done(((f32[512,512]{1,0:T(8,128)}), f32[512,512]{1,0:T(8,128)}) %all-reduce.5.cloned.1.call-update) | async-done | bytes 1048592 | tf_op jit(solution)/shard_map/psum | solution.py:75
  484.8 2.3 copy.123
  (55 shorter events, 22.7 us)
Async XLA Ops:
  7.2 76.9 %copy-start = (bf16[1,56,128,128]{3,2,1,0:T(8,128)(2,1)S(1)}, bf16[1,56,128,128]{3,2,1,0:T(8,128)(2,1)}, u32[]{:S(2)}) copy-start(bf16[1,56,128,128]{3,2,1,0:T(8,128)(2,1)} %param.8) | copy-start | bytes 5505028
  7.2 30.0 %collective-permute-start.1 = (bf16[64,2048]{1,0:T(8,128)(2,1)}, bf16[64,2048]{1,0:T(8,128)(2,1)S(1)}, u32[]{:S(2)}, u32[]{:S(2)}) collective-permute-start(bf16[64,2048]{1,0:T(8,128)(2,1)} %param.7), channel_id=1, source_target_pairs={{0,2},{1,3},{2,0},{3,1},{4,6},{5,7},{6,4},{7,5},{8,10},{9,11},{10,... | collective-permute-start | bytes 786440 | tf_op jit(solution)/shard_map/ppermute | solution.py:10
  13.1 24.1 %collective-permute-start = (bf16[64,2048]{1,0:T(8,128)(2,1)}, bf16[64,2048]{1,0:T(8,128)(2,1)S(1)}, u32[]{:S(2)}, u32[]{:S(2)}) collective-permute-start(bf16[64,2048]{1,0:T(8,128)(2,1)} %param.7), channel_id=1, source_target_pairs={{0,1},{1,0},{2,3},{3,2},{4,5},{5,4},{6,7},{7,6},{8,9},{9,8},{10,11... | collective-permute-start | bytes 786440 | tf_op jit(solution)/shard_map/ppermute | solution.py:10
  16.6 30.2 %collective-permute-start.3 = (bf16[64,2048]{1,0:T(8,128)(2,1)}, bf16[64,2048]{1,0:T(8,128)(2,1)S(1)}, u32[]{:S(2)}, u32[]{:S(2)}) collective-permute-start(bf16[64,2048]{1,0:T(8,128)(2,1)} %param.7), channel_id=1, source_target_pairs={{0,8},{1,9},{2,10},{3,11},{4,12},{5,13},{6,14},{7,15},{8,0},{9,1},... | collective-permute-start | bytes 786440 | tf_op jit(solution)/shard_map/ppermute | solution.py:10
  29.4 49.4 %collective-permute-start.2 = (bf16[64,2048]{1,0:T(8,128)(2,1)}, bf16[64,2048]{1,0:T(8,128)(2,1)S(1)}, u32[]{:S(2)}, u32[]{:S(2)}) collective-permute-start(bf16[64,2048]{1,0:T(8,128)(2,1)} %param.7), channel_id=1, source_target_pairs={{0,4},{1,5},{2,6},{3,7},{4,0},{5,1},{6,2},{7,3},{8,12},{9,13},{10,... | collective-permute-start | bytes 786440 | tf_op jit(solution)/shard_map/ppermute | solution.py:10
  84.0 1.4 copy-start.3
  85.4 6.3 %copy-start.2 = (bf16[512,256]{1,0:T(8,128)(2,1)S(1)}, bf16[512,256]{1,0:T(8,128)(2,1)}, u32[]{:S(2)}) copy-start(bf16[512,256]{1,0:T(8,128)(2,1)} %param.13) | copy-start | bytes 786436
  86.0 5.8 %copy-start.4 = (s32[1,56]{1,0:T(1,128)S(1)}, s32[1,56]{1,0:T(1,128)}, u32[]{:S(2)}) copy-start(s32[1,56]{1,0:T(1,128)} %param.10) | copy-start | bytes 676
  86.0 12.2 %copy-start.1 = (bf16[512,512]{1,0:T(8,128)(2,1)S(1)}, bf16[512,512]{1,0:T(8,128)(2,1)}, u32[]{:S(2)}) copy-start(bf16[512,512]{1,0:T(8,128)(2,1)} %param.12) | copy-start | bytes 1572868
  86.9 11.3 %all-to-all-start = ((bf16[64,8,256]{2,0,1:T(8,128)(2,1)}), bf16[64,8,256]{2,0,1:T(8,128)(2,1)S(1)}, u32[]{:S(2)}, u32[]{:S(2)}) async-start(bf16[64,8,256]{2,0,1:T(8,128)(2,1)} %copy.75), calls=%async_computation | async-start | bytes 524288 | tf_op jit(solution)/shard_map/all_to_all | solution.py:67
  100.6 10.9 %all-to-all-start.1 = ((bf16[8,64,256]{2,1,0:T(8,128)(2,1)}), bf16[8,64,256]{2,1,0:T(8,128)(2,1)S(1)}, u32[]{:S(2)}, u32[]{:S(2)}) async-start(bf16[8,64,256]{2,1,0:T(8,128)(2,1)} %bitcast.12), calls=%async_computation.1 | async-start | bytes 524288 | tf_op jit(solution)/shard_map/all_to_all | solution.py:79
  104.9 76.0 %all-reduce.3.cloned.1.call-start = ((), (), s32[]{:S(2)}) async-start(), calls=%async_computation.2 | async-start | bytes 2097152 | tf_op jit(solution)/shard_map/psum | solution.py:75
  106.2 378.6 %all-reduce.5.cloned.1.call-start = ((), (), s32[]{:S(2)}) async-start(), calls=%async_computation.3 | async-start | bytes 2097152 | tf_op jit(solution)/shard_map/psum | solution.py:75
  188.3 50.5 %slice-start = ((f32[64,5,2048]{2,1,0:T(8,128)}), f32[64,1,2048]{2,1,0:T(1,128)S(1)}, s32[]{:S(2)}) async-start(f32[64,5,2048]{2,1,0:T(8,128)} %reshape.232), calls=%async_computation.4 | async-start | bytes 1048576 | tf_op jit(solution)/shard_map/slice | solution.py:87
  189.2 30.2 %collective-permute-start.5 = (bf16[64,2048]{1,0:T(8,128)(2,1)}, bf16[64,2048]{1,0:T(8,128)(2,1)S(1)}, u32[]{:S(2)}, u32[]{:S(2)}) collective-permute-start(bf16[64,2048]{1,0:T(8,128)(2,1)} %bitcast.96), channel_id=1, source_target_pairs={{0,2},{1,3},{2,0},{3,1},{4,6},{5,7},{6,4},{7,5},{8,10},{9,11},{10,... | collective-permute-start | bytes 786440 | tf_op jit(solution)/shard_map/ppermute | solution.py:10
  192.9 37.3 %collective-permute-start.6 = (bf16[64,2048]{1,0:T(8,128)(2,1)}, bf16[64,2048]{1,0:T(8,128)(2,1)S(1)}, u32[]{:S(2)}, u32[]{:S(2)}) collective-permute-start(bf16[64,2048]{1,0:T(8,128)(2,1)} %bitcast.95), channel_id=1, source_target_pairs={{0,4},{1,5},{2,6},{3,7},{4,0},{5,1},{6,2},{7,3},{8,12},{9,13},{10,... | collective-permute-start | bytes 786440 | tf_op jit(solution)/shard_map/ppermute | solution.py:10
  200.3 30.0 %collective-permute-start.7 = (bf16[64,2048]{1,0:T(8,128)(2,1)S(1)}, bf16[64,2048]{1,0:T(8,128)(2,1)}, u32[]{:S(2)}, u32[]{:S(2)}) collective-permute-start(bf16[64,2048]{1,0:T(8,128)(2,1)S(1)} %bitcast.108), channel_id=1, source_target_pairs={{0,8},{1,9},{2,10},{3,11},{4,12},{5,13},{6,14},{7,15},{8,0},{9,1},... | collective-permute-start | bytes 786440 | tf_op jit(solution)/shard_map/ppermute | solution.py:10
  206.2 32.6 %collective-permute-start.4 = (bf16[64,2048]{1,0:T(8,128)(2,1)S(1)}, bf16[64,2048]{1,0:T(8,128)(2,1)}, u32[]{:S(2)}, u32[]{:S(2)}) collective-permute-start(bf16[64,2048]{1,0:T(8,128)(2,1)S(1)} %bitcast.107), channel_id=1, source_target_pairs={{0,1},{1,0},{2,3},{3,2},{4,5},{5,4},{6,7},{7,6},{8,9},{9,8},{10,11... | collective-permute-start | bytes 786440 | tf_op jit(solution)/shard_map/ppermute | solution.py:10
Sparse Core Ops, SparseCore 0:
  108.7 72.1 all-reduce.2
  184.3 300.4 all-reduce.4
